TPU v7x, 256 devices: a whole 4x4x8 slice. The times are simulated.
256 devices in a mesh: rows: 32 (over x, z_hi, core), feat: 8 (over y, z_lo).
Axes of the slice: x: 4, y: 4, z: 8 (z_hi: 4, z_lo: 2; z = z_hi * 2 + z_lo), core: 2. Of those that a mesh axis runs over, the one named last changes fastest.
Arguments:
- data: bfloat16 [196608, 1024], P(('rows', 'feat')), may hold values from -6 to 6
- rotation: bfloat16 [1024, 1024], P(None, 'feat'), may hold values from -0.1875 to 0.1875
- codebook: bfloat16 [256, 1024], P(None, 'feat'), may hold values from -5 to 5
Outputs:
- new_codebook: float32 [256, 1024], P(None, 'feat')
- counts: float32 [64, 256], P('feat')
- cross: float32 [1024, 1024], P('rows', 'feat')
All inputs are finite; a program needn't handle non-finite values.
Results may differ from a plain program's by a relative error of at most 0.0029.
Values may be sent and summed in bfloat16 or wider, within the bound.
No kernel may reach another device: no remote copies, remote signals or barrier semaphores. Data moves between devices by JAX's collectives and lax.ppermute only.
A program may use at most 64 MiB of HBM per device.

v0:
```python
import jax
import jax.numpy as jnp
from jax import lax
from jax.sharding import PartitionSpec as P

D = 1024
SUB = 64
inverse_temp = 0.5


def assign(grouped, code_local):
    rows_all, width = grouped.shape
    sub_width = D // SUB
    local_subs = width // sub_width
    words = code_local.shape[0]
    block = 1024
    codes = code_local.reshape(words, local_subs, sub_width)
    code_wide = code_local.astype(jnp.float32).reshape(words, local_subs, sub_width)
    squares = jnp.sum(code_wide * code_wide, axis=-1).T[:, None, :]

    def step(carry, piece):
        numer, counted = carry
        values = piece.reshape(block, local_subs, sub_width)
        dots = jnp.einsum("nsd,ksd->snk", values, codes, preferred_element_type=jnp.float32)
        logits = inverse_temp * (2.0 * dots - squares)
        weights = jax.nn.softmax(logits, axis=-1)
        weights_b = weights.astype(jnp.bfloat16)
        numer = numer + jnp.einsum(
            "snk,nsd->ksd", weights_b, values, preferred_element_type=jnp.float32
        ).reshape(words, width)
        counted = counted + jnp.sum(weights, axis=1)
        rebuilt = jnp.einsum("snk,ksd->nsd", weights_b, codes, preferred_element_type=jnp.float32)
        return ((numer, counted), rebuilt.reshape(block, width).astype(jnp.bfloat16))

    start = (jnp.zeros((words, width), jnp.float32), jnp.zeros((local_subs, words), jnp.float32))
    (numer, counted), rebuilt = lax.scan(
        step, start, grouped.reshape(rows_all // block, block, width)
    )
    return (numer, counted, rebuilt.reshape(rows_all, width))


def local(data, rotation, codebook):
    width = D
    full_rotation = lax.all_gather(rotation, "feat", axis=1, tiled=True)
    own = jnp.dot(data, full_rotation, preferred_element_type=jnp.float32).astype(jnp.bfloat16)
    grouped = lax.all_to_all(own, "feat", split_axis=1, concat_axis=0, tiled=True)
    numer, counted, rebuilt = assign(grouped, codebook)
    back = lax.all_to_all(rebuilt, "feat", split_axis=0, concat_axis=1, tiled=True)
    term = lax.dot_general(data, back, (((0,), (0,)), ((), ())), preferred_element_type=jnp.float32)
    n_rows = lax.axis_size("rows")
    n_feat = lax.axis_size("feat")
    ordered = term.reshape(n_rows, width // n_rows, n_feat, width // n_feat)
    ordered = ordered.transpose(0, 2, 1, 3).reshape(
        n_rows * n_feat * (width // n_rows), width // n_feat
    )
    cross = lax.psum_scatter(ordered, ("rows", "feat"), scatter_dimension=0, tiled=True)
    total_numer, total_counts = lax.psum((numer, counted), "rows")
    per_column = jnp.repeat(total_counts.T, D // SUB, axis=1)
    new_codebook = (total_numer + codebook.astype(jnp.float32)) / (per_column + 1.0)
    return (new_codebook, total_counts, cross)


def solution(mesh):
    in_specs = (P(("rows", "feat"), None), P(None, "feat"), P(None, "feat"))
    out_specs = (P(None, "feat"), P("feat", None), P("rows", "feat"))
    return jax.shard_map(local, mesh=mesh, in_specs=in_specs, out_specs=out_specs, check_vma=False)
```

profile of v0, /device:TPU:0, one launch (start us, length us, event | category | flops | bytes accessed | tf_op | source)
XLA Modules:
  0.0 1752.2 jit_solution(6497450159070339519)
XLA Ops:
  7.9 57.3 %all-gather.2.cloned.1.call-done = bf16[1024,1024]{1,0:T(8,128)(2,1)} async-done(((bf16[1024,128]{1,0:T(8,128)(2,1)}), bf16[1024,1024]{1,0:T(8,128)(2,1)}) %all-gather.2.cloned.1.call-update) | async-done | bytes 2097168 | tf_op jit(solution)/shard_map/all_gather | solution.py:44
  65.3 3.4 fusion.11
  68.7 1.4 copy.41
  70.1 4.4 all-to-all-start
  74.7 20.2 %all-to-all-done = bf16[768,8,128]{2,0,1:T(8,128)(2,1)} async-done(((bf16[768,8,128]{2,0,1:T(8,128)(2,1)}), bf16[768,8,128]{2,0,1:T(8,128)(2,1)}, u32[]{:S(2)}, u32[]{:S(2)}) %all-to-all-start) | async-done | bytes 1572896 | tf_op jit(solution)/shard_map/all_to_all | solution.py:46
  94.9 106.3 %while.15 = (s32[]{:T(128)}, f32[256,128]{0,1:T(8,128)S(1)}, f32[8,256]{1,0:T(8,128)S(1)}, bf16[6,1024,128]{2,1,0:T(8,128)(2,1)}, bf16[6,1024,128]{2,1,0:T(8,128...) while((s32[]{:T(128)}, f32[256,128]{0,1:T(8,128)S(1)}, ...), condition=%wide.region_5.6_spmd.clone, body=%wide.region_1.5_spmd.clone.sunk | while | flops 218302720 | bytes 49783428 | solution.py:36
  94.9 1.0 constant_dynamic-slice_fusion.2
  96.0 5.5 fusion.42
  101.5 4.2 fusion.43
  105.7 1.9 copy-done.1
  107.6 1.2 fusion.44
  108.8 2.8 convolution_convert_fusion.3
  112.6 1.0 constant_dynamic-slice_fusion.2
  113.7 5.5 fusion.42
  119.2 4.2 fusion.43
  123.4 1.9 copy-done.1
  125.3 1.2 fusion.44
  126.5 2.8 convolution_convert_fusion.3
  131.4 5.5 fusion.42
  136.9 4.2 fusion.43
  141.1 1.9 copy-done.1
  143.0 1.2 fusion.44
  144.2 2.8 convolution_convert_fusion.3
  149.2 5.5 fusion.42
  154.6 4.2 fusion.43
  158.8 1.9 copy-done.1
  160.8 1.2 fusion.44
  162.0 2.8 convolution_convert_fusion.3
  166.9 5.5 fusion.42
  172.4 4.2 fusion.43
  176.6 1.9 copy-done.1
  178.5 1.2 fusion.44
  179.7 2.8 convolution_convert_fusion.3
  184.6 5.5 fusion.42
  190.1 4.2 fusion.43
  194.3 1.9 copy-done.1
  196.2 1.2 fusion.44
  197.4 2.8 convolution_convert_fusion.3
  201.2 3.6 all-to-all-start.1
  205.6 19.5 %all-to-all-done.1 = bf16[8,768,128]{2,1,0:T(8,128)(2,1)S(1)} async-done(((bf16[8,768,128]{2,1,0:T(8,128)(2,1)}), bf16[8,768,128]{2,1,0:T(8,128)(2,1)S(1)}, u32[]{:S(2)}, u32[]{:S(2)}) %all-to-all-start.1) | async-done | bytes 1572896 | tf_op jit(solution)/shard_map/all_to_all | solution.py:48
  225.1 1.6 copy.29
  226.6 5.1 convolution_bitcast_fusion
  231.8 5.4 copy.30
  237.2 3.2 copy.39
  240.8 2.7 copy.31
  243.6 70.9 %psum.15 = f32[8,256]{1,0:T(8,128)S(1)} all-reduce(f32[8,256]{1,0:T(8,128)S(1)} %get-tuple-element.43), channel_id=1, replica_groups=mesh['rows'=32,'feat'=8] {'rows'}, use_global_device_ids=true, to_apply=%region_7.8 | all-reduce | flops 2048 | bytes 16384 | tf_op jit(solution)/shard_map/psum | solution.py:57
  314.5 155.2 %all-reduce.2.cloned.1.call-done = f32[256,128]{0,1:T(8,128)} async-done(((f32[256,128]{0,1:T(8,128)}), f32[256,128]{0,1:T(8,128)}) %all-reduce.2.cloned.1.call-update) | async-done | bytes 131088 | tf_op jit(solution)/shard_map/psum | solution.py:57
  471.4 1274.3 %reduce-scatter.2.cloned.1.call-done = f32[32,128]{1,0:T(8,128)} async-done(((f32[8192,128]{1,0:T(8,128)}), f32[32,128]{1,0:T(8,128)}) %reduce-scatter.2.cloned.1.call-update) | async-done | bytes 16400 | tf_op jit(solution)/shard_map/reduce_scatter | solution.py:56
  (63 shorter events, 14.3 us)
Async XLA Ops:
  7.2 58.1 %copy-start = (bf16[768,1024]{1,0:T(8,128)(2,1)S(1)}, bf16[768,1024]{1,0:T(8,128)(2,1)}, u32[]{:S(2)}) copy-start(bf16[768,1024]{1,0:T(8,128)(2,1)} %param.5) | copy-start | bytes 4718596
  7.2 58.1 %all-gather.2.cloned.1.call-start = ((), (), s32[]{:S(2)}) async-start(), calls=%async_computation.3 | async-start | bytes 2359296 | tf_op jit(solution)/shard_map/all_gather | solution.py:44
  68.6 5.9 copy-start.3
  70.1 24.8 %all-to-all-start = ((bf16[768,8,128]{2,0,1:T(8,128)(2,1)}), bf16[768,8,128]{2,0,1:T(8,128)(2,1)}, u32[]{:S(2)}, u32[]{:S(2)}) async-start(bf16[768,8,128]{2,0,1:T(8,128)(2,1)} %bitcast.50), calls=%async_computation | async-start | bytes 3145728 | tf_op jit(solution)/shard_map/all_to_all | solution.py:46
  105.7 1.9 copy-start.1
  123.4 1.9 copy-start.1
  141.1 1.9 copy-start.1
  158.8 1.9 copy-start.1
  176.6 1.9 copy-start.1
  194.3 1.9 copy-start.1
  201.2 3.6 copy-start.2
  201.2 23.9 %all-to-all-start.1 = ((bf16[8,768,128]{2,1,0:T(8,128)(2,1)}), bf16[8,768,128]{2,1,0:T(8,128)(2,1)S(1)}, u32[]{:S(2)}, u32[]{:S(2)}) async-start(bf16[8,768,128]{2,1,0:T(8,128)(2,1)} %bitcast.81), calls=%async_computation.1 | async-start | bytes 3145728 | tf_op jit(solution)/shard_map/all_to_all | solution.py:48
  204.8 264.9 %all-reduce.2.cloned.1.call-start = ((), (), s32[]{:S(2)}) async-start(), calls=%async_computation.4 | async-start | bytes 262144 | tf_op jit(solution)/shard_map/psum | solution.py:57
  205.5 1540.1 %reduce-scatter.2.cloned.1.call-start = ((), (), s32[]{:S(2)}) async-start(), calls=%async_computation.5 | async-start | bytes 4210688 | tf_op jit(solution)/shard_map/reduce_scatter | solution.py:56
  314.4 1431.2 %copy-start.4 = (f32[8,256]{1,0:T(8,128)}, f32[8,256]{1,0:T(8,128)S(1)}, u32[]{:S(2)}) copy-start(f32[8,256]{1,0:T(8,128)S(1)} %psum.15) | copy-start | bytes 24580
Sparse Core Ops, SparseCore 0:
  9.7 55.4 all-gather.1
  208.8 260.8 all-reduce.1
  472.9 1272.7 reduce-scatter.1
where the time goes:
time: 1750 us
  waiting for transfers between devices  1530 us (87%)
  blocking collectives  70.9 us (4%)
  matrix products  65.5 us (4%)
  local copies, waits for them, and re-layouts  39.4 us (2%)
  other arithmetic  26.3 us (2%)
    reduce_scatter x1, waiting for transfers between devices, local(): lax.psum_scatter(ordered, ('rows', 'feat'), scatter_dimension=0, tiled=True)  1270 us
    psum x1, waiting for transfers between devices, local(): total_numer, total_counts = lax.psum((numer, counted), 'rows')  155 us
    psum x1, blocking collectives, local(): total_numer, total_counts = lax.psum((numer, counted), 'rows')  70.9 us
    all_gather x1, waiting for transfers between devices, local(): full_rotation = lax.all_gather(rotation, 'feat', axis=1, tiled=True)  57.3 us
  transfers between devices with their start and end apart: 5, of which 5 were waited for; matrix products, arithmetic and copies ran while one was open for 1% of the time, Pallas kernels for 0%

commit v1 on v0

--- a/solution.py
+++ b/solution.py
@@ -41,7 +41,16 @@
 
 def local(data, rotation, codebook):
     width = D
-    full_rotation = lax.all_gather(rotation, "feat", axis=1, tiled=True)
+    object_advance = lambda here_x, along_axis: jnp.concatenate(
+        lax.all_to_all(
+            jnp.stack([here_x] * lax.psum(1, along_axis), axis=0),
+            axis_name=along_axis,
+            split_axis=0,
+            concat_axis=0,
+        ),
+        1,
+    )
+    full_rotation = object_advance(rotation, along_axis="feat")
     own = jnp.dot(data, full_rotation, preferred_element_type=jnp.float32).astype(jnp.bfloat16)
     grouped = lax.all_to_all(own, "feat", split_axis=1, concat_axis=0, tiled=True)
     numer, counted, rebuilt = assign(grouped, codebook)

time: 1750 us -> 1500 us (0.86)
  waiting for transfers between devices: 1530 us -> 1240 us
  blocking collectives: 70.9 us -> 107 us
    reduce_scatter x1, waiting for transfers between devices: 1270 us -> 1050 us  [local(): lax.psum_scatter(ordered, ('rows', 'feat'), scatter_dimension=0, tiled=True)]
    all_gather x1 -> x0, waiting for transfers between devices: 57.3 us -> none  [local(): full_rotation = lax.all_gather(rotation, 'feat', axis=1, tiled=True)]
    all_to_all x0 -> x1, blocking collectives: none -> 31.1 us  [local(): lax.all_to_all(jnp.stack([here_x] * lax.psum(1, along_axis), axis=0), axi...]
  transfers between devices with their start and end apart: 5 -> 4, of which waited for: 5 -> 4; matrix products, arithmetic and copies ran while one was open for 1% -> 1% of each run, Pallas kernels for 0% -> 0%
where the time goes in v1:
time: 1500 us
  waiting for transfers between devices  1240 us (83%)
  blocking collectives  107 us (7%)
  matrix products  64 us (4%)
  local copies, waits for them, and re-layouts  40.7 us (3%)
  other arithmetic  26.3 us (2%)
  between operations  15.6 us (1%)
    reduce_scatter x1, waiting for transfers between devices, local(): lax.psum_scatter(ordered, ('rows', 'feat'), scatter_dimension=0, tiled=True)  1050 us
    psum x1, waiting for transfers between devices, local(): total_numer, total_counts = lax.psum((numer, counted), 'rows')  153 us
    psum x1, blocking collectives, local(): total_numer, total_counts = lax.psum((numer, counted), 'rows')  75.8 us
    sub x6, matrix products, step(): weights = jax.nn.softmax(logits, axis=-1)  32.9 us
    all_to_all x1, blocking collectives, local(): lax.all_to_all(jnp.stack([here_x] * lax.psum(1, along_axis), axis=0), axi...  31.1 us
  transfers between devices with their start and end apart: 4, of which 4 were waited for; matrix products, arithmetic and copies ran while one was open for 1% of the time, Pallas kernels for 0%

profile of v1, /device:TPU:0, one launch (start us, length us, event | category | flops | bytes accessed | tf_op | source)
XLA Modules:
  0.0 1503.0 jit_solution(2880537556014882394)
XLA Ops:
  8.0 1.2 copy.25
  9.5 31.1 %all_to_all.40 = bf16[8,1024,128]{1,2,0:T(8,128)(2,1)S(1)} all-to-all(bf16[8,1024,128]{1,2,0:T(8,128)(2,1)S(1)} %stack.2), channel_id=1, replica_groups=mesh['rows'=32,'feat'=8] {'feat'}, dimensions={0} | all-to-all | bytes 4194304 | tf_op jit(solution)/shard_map/all_to_all | solution.py:45
  40.6 1.8 fusion.11
  42.5 1.4 copy.43
  43.9 4.3 all-to-all-start.1
  48.4 20.2 %all-to-all-done.1 = bf16[768,8,128]{2,0,1:T(8,128)(2,1)} async-done(((bf16[768,8,128]{2,0,1:T(8,128)(2,1)}), bf16[768,8,128]{2,0,1:T(8,128)(2,1)}, u32[]{:S(2)}, u32[]{:S(2)}) %all-to-all-start.1) | async-done | bytes 1572896 | tf_op jit(solution)/shard_map/all_to_all | solution.py:55
  68.6 106.2 %while.15 = (s32[]{:T(128)}, f32[256,128]{0,1:T(8,128)S(1)}, f32[8,256]{1,0:T(8,128)S(1)}, bf16[6,1024,128]{2,1,0:T(8,128)(2,1)}, bf16[6,1024,128]{2,1,0:T(8,128...) while((s32[]{:T(128)}, f32[256,128]{0,1:T(8,128)S(1)}, ...), condition=%wide.region_5.6_spmd.clone, body=%wide.region_1.5_spmd.clone.sunk | while | flops 218302720 | bytes 49783428 | solution.py:36
  68.6 1.0 constant_dynamic-slice_fusion.2
  69.8 5.5 fusion.42
  75.2 4.2 fusion.43
  79.4 1.9 copy-done.1
  81.3 1.2 fusion.44
  82.6 2.8 convolution_convert_fusion.3
  87.5 5.5 fusion.42
  92.9 4.2 fusion.43
  97.1 1.9 copy-done.1
  99.1 1.2 fusion.44
  100.3 2.8 convolution_convert_fusion.3
  105.2 5.5 fusion.42
  110.7 4.2 fusion.43
  114.8 1.9 copy-done.1
  116.8 1.2 fusion.44
  118.0 2.8 convolution_convert_fusion.3
  122.9 5.5 fusion.42
  128.4 4.2 fusion.43
  132.6 1.9 copy-done.1
  134.5 1.2 fusion.44
  135.7 2.8 convolution_convert_fusion.3
  140.6 5.5 fusion.42
  146.1 4.2 fusion.43
  150.3 1.9 copy-done.1
  152.2 1.2 fusion.44
  153.4 2.8 convolution_convert_fusion.3
  158.3 5.5 fusion.42
  163.8 4.2 fusion.43
  168.0 1.9 copy-done.1
  169.9 1.2 fusion.44
  171.1 2.8 convolution_convert_fusion.3
  174.9 3.6 all-to-all-start.2
  179.3 19.7 %all-to-all-done.2 = bf16[8,768,128]{2,1,0:T(8,128)(2,1)S(1)} async-done(((bf16[8,768,128]{2,1,0:T(8,128)(2,1)}), bf16[8,768,128]{2,1,0:T(8,128)(2,1)S(1)}, u32[]{:S(2)}, u32[]{:S(2)}) %all-to-all-start.2) | async-done | bytes 1572896 | tf_op jit(solution)/shard_map/all_to_all | solution.py:57
  199.0 1.6 copy.31
  200.6 5.1 convolution_bitcast_fusion
  205.7 5.4 copy.32
  211.0 3.2 copy.41
  214.7 2.7 copy.33
  217.4 75.8 %psum.15 = f32[8,256]{1,0:T(8,128)S(1)} all-reduce(f32[8,256]{1,0:T(8,128)S(1)} %get-tuple-element.43), channel_id=1, replica_groups=mesh['rows'=32,'feat'=8] {'rows'}, use_global_device_ids=true, to_apply=%region_7.8 | all-reduce | flops 2048 | bytes 16384 | tf_op jit(solution)/shard_map/psum | solution.py:66
  293.3 153.0 %all-reduce.2.cloned.1.call-done = f32[256,128]{0,1:T(8,128)} async-done(((f32[256,128]{0,1:T(8,128)}), f32[256,128]{0,1:T(8,128)}) %all-reduce.2.cloned.1.call-update) | async-done | bytes 131088 | tf_op jit(solution)/shard_map/psum | solution.py:66
  447.9 1047.6 %reduce-scatter.2.cloned.1.call-done = f32[32,128]{1,0:T(8,128)} async-done(((f32[8192,128]{1,0:T(8,128)}), f32[32,128]{1,0:T(8,128)}) %reduce-scatter.2.cloned.1.call-update) | async-done | bytes 16400 | tf_op jit(solution)/shard_map/reduce_scatter | solution.py:65
  (63 shorter events, 14.8 us)
Async XLA Ops:
  8.0 32.6 %copy-start = (bf16[768,1024]{1,0:T(8,128)(2,1)S(1)}, bf16[768,1024]{1,0:T(8,128)(2,1)}, u32[]{:S(2)}) copy-start(bf16[768,1024]{1,0:T(8,128)(2,1)} %param.5) | copy-start | bytes 4718596
  42.5 5.8 copy-start.3
  43.9 24.7 %all-to-all-start.1 = ((bf16[768,8,128]{2,0,1:T(8,128)(2,1)}), bf16[768,8,128]{2,0,1:T(8,128)(2,1)}, u32[]{:S(2)}, u32[]{:S(2)}) async-start(bf16[768,8,128]{2,0,1:T(8,128)(2,1)} %bitcast.53), calls=%async_computation.1 | async-start | bytes 3145728 | tf_op jit(solution)/shard_map/all_to_all | solution.py:55
  79.4 1.9 copy-start.1
  97.1 1.9 copy-start.1
  114.8 1.9 copy-start.1
  132.5 1.9 copy-start.1
  150.3 1.9 copy-start.1
  168.0 1.9 copy-start.1
  174.9 3.6 copy-start.2
  174.9 24.1 %all-to-all-start.2 = ((bf16[8,768,128]{2,1,0:T(8,128)(2,1)}), bf16[8,768,128]{2,1,0:T(8,128)(2,1)S(1)}, u32[]{:S(2)}, u32[]{:S(2)}) async-start(bf16[8,768,128]{2,1,0:T(8,128)(2,1)} %bitcast.85), calls=%async_computation.2 | async-start | bytes 3145728 | tf_op jit(solution)/shard_map/all_to_all | solution.py:57
  178.5 267.8 %all-reduce.2.cloned.1.call-start = ((), (), s32[]{:S(2)}) async-start(), calls=%async_computation.4 | async-start | bytes 262144 | tf_op jit(solution)/shard_map/psum | solution.py:66
  179.2 1316.3 %reduce-scatter.2.cloned.1.call-start = ((), (), s32[]{:S(2)}) async-start(), calls=%async_computation.5 | async-start | bytes 4210688 | tf_op jit(solution)/shard_map/reduce_scatter | solution.py:65
  293.2 1202.3 %copy-start.4 = (f32[8,256]{1,0:T(8,128)}, f32[8,256]{1,0:T(8,128)S(1)}, u32[]{:S(2)}) copy-start(f32[8,256]{1,0:T(8,128)S(1)} %psum.15) | copy-start | bytes 24580
Sparse Core Ops, SparseCore 0:
  182.5 263.6 all-reduce.1
Sparse Core Ops, SparseCore 1:
  217.5 1278.0 reduce-scatter.1
